TPU v7x, 32 devices: a whole 2x2x4 slice. The times are simulated.
32 devices in a mesh: space: 8 (over y, x, core), orb: 4 (over z).
Axes of the slice: x: 2, y: 2, z: 4, core: 2. Of those that a mesh axis runs over, the one named last changes fastest.
Arguments:
- wavefunctions: float32 [8, 1536, 384], P('space', None, 'orb'), may hold values from -70 to 70
- cell_ham: float32 [8, 4, 729, 729], P('space'), may hold values from -1 to 1, as said below
- cell_nodes: int32 [8, 4, 729], P('space'), may hold values from 0 to 1535, as said below
- cell_count: int32 [8], P('space'), may hold values from 2 to 4, as said below
- upper_nodes: int32 [8, 512], P('space'), may hold values from 0 to 1536, as said below
- lower_nodes: int32 [8, 512], P('space'), may hold values from 0 to 1536, as said below
Outputs:
- rotated: float32 [8, 1536, 384], P('space', 'orb')
Inputs may be any that keep to these rules, and one draw needn't show every extreme that they name: `cell_nodes`: each cell's 729 entries are distinct. `cell_count`: some part has 4 live cells. Entries equal to 1536 are empty slots and come after the live ones; for p < 7, upper_nodes[p, k] is live exactly where lower_nodes[p + 1, k] is, and the two name the same shared node; the live entries of upper_nodes[p] and lower_nodes[p] are all distinct; the last part's list is empty; some list has all 512 slots live. `lower_nodes`: paired with upper_nodes as stated there; the first part's list is empty. `cell_ham`: each cell's matrix is symmetric.
All inputs are finite; a program needn't handle non-finite values.
Results may differ from a plain program's by a relative error of at most 0.0003.
Values sent between devices are 32-bit elements; how exact they have to be, the bound alone decides.
A program may use at most 64 MiB of HBM per device.

v0:
```python
import functools

import jax
import jax.numpy as jnp
from jax import lax
from jax.experimental import pallas as pl
from jax.experimental.pallas import tpu as pltpu
from jax.sharding import PartitionSpec as P

DEGREE = 3
LANES = 128
GROUP = 8
MESH = pl.DeviceIdType.MESH


center_shift = 0.5
half_width = 2.0


def split(values):
    high = values.astype(jnp.bfloat16)
    return high, (values - high.astype(jnp.float32)).astype(jnp.bfloat16)


def plain_dot(left, right):
    return lax.dot_general(left, right, (((1,), (0,)), ((), ())), preferred_element_type=jnp.float32)


def folded(product):
    return product[:, :LANES] + product[:, LANES:]


def filter_kernel(n_space, degree, start, matrices, node_row, list_row, out, gather, scatter, pick, place, stack,
                  fields, packed, cell_out, sums, outgoing, arriving, load_sem, send_sem, recv_sem):
    space = lax.axis_index("space")
    nodes, width = start.shape
    cells, doubled, cell_size = stack.shape
    slots = list_row.shape[1] // 2
    has_above, has_below = space < n_space - 1, space > 0

    for cell in range(cells):
        pltpu.make_async_copy(matrices.at[cell], stack.at[cell], load_sem.at[cell]).start()
    arriving[...] = jnp.zeros_like(arriving)

    barrier = pltpu.get_barrier_semaphore()

    @pl.when(has_above)
    def _():
        pl.semaphore_signal(barrier, inc=1, device_id={"space": space + 1}, device_id_type=MESH)

    @pl.when(has_below)
    def _():
        pl.semaphore_signal(barrier, inc=1, device_id={"space": space - 1}, device_id_type=MESH)

    lane = lax.broadcasted_iota(jnp.int32, (LANES, LANES), 1).astype(jnp.float32)
    sublane = lax.broadcasted_iota(jnp.int32, (LANES, LANES), 0).astype(jnp.float32)

    def ones_where(condition):
        return jnp.where(condition, 1.0, 0.0).astype(jnp.bfloat16)

    def tile_at(index):
        return pl.ds(pl.multiple_of(index * LANES, LANES), LANES)

    def upright(row):
        return jnp.transpose(jnp.broadcast_to(row, (LANES, LANES)))

    def gather_rows(chunk, carry):
        here = tile_at(chunk)
        column = upright(node_row[:, here])
        for tile in range(nodes // LANES):
            gather[here, tile * LANES : (tile + 1) * LANES] = ones_where(column == lane + float(tile * LANES))
        return carry

    def pick_rows(chunk, carry):
        here = tile_at(chunk)
        column = upright(list_row[:, here])
        for tile in range(node_row.shape[1] // LANES):
            there = slice(tile * LANES, (tile + 1) * LANES)
            pick[here, there] = ones_where(column == node_row[:, there])
        return carry

    def node_rows(chunk, carry):
        here = tile_at(chunk)
        node = sublane + (chunk * LANES).astype(jnp.float32)
        for tile in range(node_row.shape[1] // LANES):
            there = slice(tile * LANES, (tile + 1) * LANES)
            scatter[here, there] = ones_where(node == node_row[:, there])
        for tile in range(2 * slots // LANES):
            there = slice(tile * LANES, (tile + 1) * LANES)
            other = (tile * LANES + slots) % (2 * slots)
            place[here, there] = ones_where(node == list_row[:, other : other + LANES])
        values = jnp.concatenate([start[here, :], jnp.zeros((LANES, LANES - width), jnp.float32)], axis=1)
        fields[0, here, :] = values
        fields[1, here, :] = values
        high, low = split(values)
        packed[here, :LANES] = high
        packed[here, LANES:] = low
        return carry

    lax.fori_loop(0, node_row.shape[1] // LANES, gather_rows, 0)
    lax.fori_loop(0, 2 * slots // LANES, pick_rows, 0)
    lax.fori_loop(0, nodes // LANES, node_rows, 0)
    for cell in range(cells):
        pltpu.make_async_copy(matrices.at[cell], stack.at[cell], load_sem.at[cell]).wait()
    pl.semaphore_wait(barrier, has_above.astype(jnp.int32) + has_below.astype(jnp.int32))

    part = nodes // 3 if nodes % (3 * LANES) == 0 else LANES

    def apply(step, carry):
        def one_cell(cell, carry):
            here = pl.ds(pl.multiple_of(cell * cell_size, LANES), cell_size)
            local = plain_dot(gather[here, :], packed[...]).astype(jnp.bfloat16)
            high_part = plain_dot(stack[cell, :cell_size, :], local)
            low_part = plain_dot(stack[cell, cell_size:, :], local[:, :LANES])
            high, low = split(folded(high_part) + low_part)
            cell_out[here, :LANES] = high
            cell_out[here, LANES:] = low
            return carry

        lax.fori_loop(0, cells, one_cell, 0)

        def transfer(way, towards):
            return pltpu.make_async_remote_copy(
                src_ref=outgoing.at[way],
                dst_ref=arriving.at[step, way],
                send_sem=send_sem.at[step, way],
                recv_sem=recv_sem.at[step, way],
                device_id={"space": towards},
                device_id_type=MESH,
            )

        down, up = transfer(0, space - 1), transfer(1, space + 1)
        outgoing[0] = folded(plain_dot(pick[:slots, :], cell_out[...]))

        @pl.when(has_below)
        def _():
            down.start()

        outgoing[1] = folded(plain_dot(pick[slots:, :], cell_out[...]))

        @pl.when(has_above)
        def _():
            up.start()

        def node_sums(chunk, carry):
            here = pl.ds(pl.multiple_of(chunk * part, LANES), part)
            sums[here, :] = folded(plain_dot(scatter[here, :], cell_out[...]))
            return carry

        lax.fori_loop(0, nodes // part, node_sums, 0)

        @pl.when(has_below)
        def _():
            down.wait_send()
            up.wait_recv()

        @pl.when(has_above)
        def _():
            up.wait_send()
            down.wait_recv()

        new, old = lax.rem(step + 1, 2), lax.rem(step, 2)
        first = step == 0
        scale = jnp.where(first, 1.0 / half_width, 2.0 / half_width)
        keep = jnp.where(first, 0.0, 1.0)
        parts = [split(arriving[step, way]) for way in range(2)]
        arrived = jnp.concatenate([jnp.concatenate(pair, axis=1) for pair in parts], axis=0)

        def advance(chunk, carry):
            here = pl.ds(pl.multiple_of(chunk * part, LANES), part)
            total = sums[here, :] + folded(plain_dot(place[here, :], arrived))
            value = scale * (total - center_shift * fields[old, here, :]) - keep * fields[new, here, :]
            fields[new, here, :] = value
            high, low = split(value)
            packed[here, :LANES] = high
            packed[here, LANES:] = low
            return carry

        lax.fori_loop(0, nodes // part, advance, 0)
        return carry

    lax.fori_loop(0, degree, apply, 0)
    out[...] = fields[degree % 2, :, :width]


def filtered_block(start, matrices, node_map, live_cells, upper_list, lower_list, n_space):
    nodes, width = start.shape
    cells, cell_nodes = node_map.shape
    cell_size = -(-cell_nodes // LANES) * LANES
    room = cell_size - cell_nodes
    slots = upper_list.shape[0]

    high = lax.reduce_precision(matrices, exponent_bits=8, mantissa_bits=7)
    margin = ((0, 0), (0, room), (0, room))
    stack = jnp.concatenate(
        [jnp.pad(piece.astype(jnp.bfloat16), margin) for piece in (high, matrices - high)], axis=1
    )
    live = jnp.arange(cells)[:, None] < live_cells
    node_row = jnp.pad(jnp.where(live, node_map, -1), ((0, 0), (0, room)), constant_values=-1)
    node_row = node_row.reshape(1, cells * cell_size).astype(jnp.float32)
    list_row = jnp.concatenate([lower_list, upper_list]).reshape(1, 2 * slots).astype(jnp.float32)

    vmem, anywhere = pl.BlockSpec(memory_space=pltpu.VMEM), pl.BlockSpec(memory_space=pl.ANY)
    dma = pltpu.SemaphoreType.DMA
    every, half = jnp.float32, jnp.bfloat16
    return pl.pallas_call(
        functools.partial(filter_kernel, n_space, DEGREE),
        out_shape=jax.ShapeDtypeStruct(start.shape, jnp.float32),
        in_specs=[vmem, anywhere, vmem, vmem],
        out_specs=vmem,
        scratch_shapes=[
            pltpu.VMEM((cells * cell_size, nodes), half),
            pltpu.VMEM((nodes, cells * cell_size), half),
            pltpu.VMEM((2 * slots, cells * cell_size), half),
            pltpu.VMEM((nodes, 2 * slots), half),
            pltpu.VMEM((cells, 2 * cell_size, cell_size), half),
            pltpu.VMEM((2, nodes, LANES), every),
            pltpu.VMEM((nodes, 2 * LANES), half),
            pltpu.VMEM((cells * cell_size, 2 * LANES), half),
            pltpu.VMEM((nodes, LANES), every),
            pltpu.VMEM((2, slots, LANES), every),
            pltpu.VMEM((DEGREE, 2, slots, LANES), every),
            dma((cells,)),
            dma((DEGREE, 2)),
            dma((DEGREE, 2)),
        ],
        compiler_params=pltpu.CompilerParams(
            collective_id=2, has_side_effects=True, vmem_limit_bytes=58 * 2**20
        ),
        name="filter",
    )(start, stack, node_row, list_row)


def exact_dot(left, right, dims):
    return lax.dot_general(
        left,
        right,
        (dims, ((), ())),
        precision=lax.Precision.HIGHEST,
        preferred_element_type=jnp.float32,
    )


def block_pairs(blocks):
    return [(i, j) for i in range(blocks) for j in range(i + 1)]


def gram_kernel(n_space, n_orb, inside, field, lower_list, rows_out, gram_out, pieces, local, parts, slab, others,
                turn_send, turn_recv, split_send, split_recv, orb_send, orb_recv, join_send, join_recv):
    space, orb = lax.axis_index("space"), lax.axis_index("orb")
    node_total, width = field.shape
    quarter = node_total // n_orb
    columns = width * n_orb
    partners = n_orb - 1

    barrier = pltpu.get_barrier_semaphore()
    for step in range(1, n_orb):
        pl.semaphore_signal(barrier, inc=1, device_id={"orb": lax.rem(orb + step, n_orb)}, device_id_type=MESH)
    if inside:
        partners += n_space - 1
        for step in range(1, n_space):
            pl.semaphore_signal(barrier, inc=1, device_id={"space": lax.rem(space + step, n_space)}, device_id_type=MESH)
    pl.semaphore_wait(barrier, partners)

    def exchange(axis, size, here, send_sems, recv_sems, source, target):
        copies = []
        for step in range(1, size):
            other = lax.rem(here + step, size)
            copy = pltpu.make_async_remote_copy(
                src_ref=source(other),
                dst_ref=target,
                send_sem=send_sems.at[step],
                recv_sem=recv_sems.at[step],
                device_id={axis: other},
                device_id_type=MESH,
            )
            copy.start()
            copies.append(copy)
        return copies

    def own_quarter(which):
        return field.at[pl.ds(pl.multiple_of(which * quarter, 8), quarter)]

    copies = exchange("orb", n_orb, orb, turn_send, turn_recv, own_quarter, pieces.at[orb])
    pieces[orb] = field[pl.ds(pl.multiple_of(orb * quarter, 8), quarter), :]
    node = lax.broadcasted_iota(jnp.int32, (quarter, lower_list.shape[1]), 0) + orb * quarter
    hits = jnp.where(node == lower_list[...], 1.0, 0.0)
    weight = (1.0 - jnp.max(hits, axis=1, keepdims=True)) * (1.0 / (n_space * node_total))
    for copy in copies:
        copy.wait()
    for which in range(n_orb):
        rows_out[:, which * width : (which + 1) * width] = pieces[which]

    blocks = columns // LANES
    for spot, (i, j) in enumerate(block_pairs(blocks)):
        left = rows_out[:, i * LANES : (i + 1) * LANES] * weight
        right = rows_out[:, j * LANES : (j + 1) * LANES]
        term = exact_dot(left, right, ((0,), (0,)))
        if inside:
            local[spot * LANES : (spot + 1) * LANES, :] = term
        else:
            gram_out[spot * LANES : (spot + 1) * LANES, :] = term
    if not inside:
        return

    chunk = local.shape[0] // n_space

    def chunk_of(which):
        return local.at[pl.ds(pl.multiple_of(which * chunk, 8), chunk)]

    copies = exchange("space", n_space, space, split_send, split_recv, chunk_of, parts.at[space])
    parts[space] = local[pl.ds(pl.multiple_of(space * chunk, 8), chunk), :]
    for copy in copies:
        copy.wait()
    slab[...] = jnp.sum(parts[...], axis=0)

    copies = exchange("orb", n_orb, orb, orb_send, orb_recv, lambda _: slab, others.at[orb])
    others[orb] = slab[...]
    for copy in copies:
        copy.wait()
    mine = pl.ds(pl.multiple_of(space * chunk, 8), chunk)
    gram_out[mine, :] = jnp.sum(others[...], axis=0)
    copies = exchange("space", n_space, space, join_send, join_recv, lambda _: gram_out.at[mine], gram_out.at[mine])
    for copy in copies:
        copy.wait()


def turn_and_gram(field, lower_list, n_space, n_orb):
    node_total, width = field.shape
    quarter, columns = node_total // n_orb, width * n_orb
    packed = len(block_pairs(columns // LANES)) * LANES
    inside = n_space <= 8 and packed % (8 * n_space) == 0
    groups = n_space if inside else 1
    chunk = packed // groups
    dma = pltpu.SemaphoreType.DMA
    vmem = pl.BlockSpec(memory_space=pltpu.VMEM)
    rows, gram = pl.pallas_call(
        functools.partial(gram_kernel, n_space, n_orb, inside),
        out_shape=(
            jax.ShapeDtypeStruct((quarter, columns), jnp.float32),
            jax.ShapeDtypeStruct((packed, LANES), jnp.float32),
        ),
        in_specs=[vmem, vmem],
        out_specs=(vmem, vmem),
        scratch_shapes=[
            pltpu.VMEM((n_orb, quarter, width), jnp.float32),
            pltpu.VMEM((packed, LANES), jnp.float32),
            pltpu.VMEM((groups, chunk, LANES), jnp.float32),
            pltpu.VMEM((chunk, LANES), jnp.float32),
            pltpu.VMEM((n_orb, chunk, LANES), jnp.float32),
            dma((n_orb,)), dma((n_orb,)),
            dma((groups,)), dma((groups,)),
            dma((n_orb,)), dma((n_orb,)),
            dma((groups,)), dma((groups,)),
        ],
        compiler_params=pltpu.CompilerParams(
            collective_id=1, has_side_effects=True, vmem_limit_bytes=40 * 2**20
        ),
        name="turn_and_gram",
    )(field, lower_list)
    if not inside:
        gram = lax.psum(gram, ("space", "orb"))
    return rows, gram


def invert_factor(matrix, inverse):
    size = matrix.shape[0]
    row_id = lax.broadcasted_iota(jnp.int32, (size, size), 0)
    column_id = lax.broadcasted_iota(jnp.int32, (size, size), 1)
    inverse[...] = jnp.where(row_id == column_id, 1.0, 0.0)
    for start in range(0, size, GROUP):
        below = start + GROUP
        rows = [matrix[start + b : start + b + 1, :] for b in range(GROUP)]
        eyes = [inverse[start + b : start + b + 1, :] for b in range(GROUP)]
        entry = {
            (b, c): jnp.broadcast_to(rows[b][:, start + c : start + c + 1], (1, size))
            for b in range(GROUP)
            for c in range(b + 1)
        }
        lower, scale, done = {}, [], []
        for b in range(GROUP):
            scale.append(lax.rsqrt(entry[b, b]))
            for i in range(b + 1, GROUP):
                lower[i, b] = entry[i, b] * scale[b]
            for i in range(b + 1, GROUP):
                for j in range(b + 1, i + 1):
                    entry[i, j] = entry[i, j] - lower[i, b] * lower[j, b]
            done.append((rows[b] * scale[b], eyes[b] * scale[b]))
            for i in range(b + 1, GROUP):
                rows[i] = rows[i] - lower[i, b] * done[b][0]
                eyes[i] = eyes[i] - lower[i, b] * done[b][1]
        for b in range(GROUP):
            inverse[start + b : start + b + 1, :] = done[b][1]
        if below == size:
            break
        back = list(done)
        for b in reversed(range(GROUP)):
            back[b] = (back[b][0] * scale[b], back[b][1] * scale[b])
            for i in range(b):
                back[i] = (back[i][0] - lower[b, i] * back[b][0], back[i][1] - lower[b, i] * back[b][1])
        rest = matrix[below:, :]
        rest_eye = inverse[below:, :]
        raw = [jnp.broadcast_to(rest[:, start + c : start + c + 1], rest.shape) for c in range(GROUP)]
        for c in range(GROUP):
            rest = rest - raw[c] * back[c][0]
            rest_eye = rest_eye - raw[c] * back[c][1]
        matrix[below:, :] = rest
        inverse[below:, :] = rest_eye


def rotate_kernel(rows, gram, rotated, lower, block, inverse):
    columns = rows.shape[1]
    blocks = columns // LANES
    lower[...] = jnp.zeros_like(lower)
    rotated[...] = jnp.zeros_like(rotated)
    last, second = ((1,), (1,)), ((1,), (1,))

    def one_block(k, carry):
        here = pl.ds(pl.multiple_of(k * LANES, LANES), LANES)
        spot = (k * (k + 3)) // 2
        own = lower[k]
        diagonal = gram[pl.ds(pl.multiple_of(spot * LANES, LANES), LANES), :]
        block[...] = diagonal - exact_dot(own, own, last)
        invert_factor(block, inverse)
        for i in range(1, blocks):

            @pl.when(i > k)
            def _():
                at = (i * (i + 1)) // 2 + k
                under = gram[pl.ds(pl.multiple_of(at * LANES, LANES), LANES), :]
                under = under - exact_dot(lower[i], own, last)
                lower[i, :, here] = exact_dot(under, inverse[...], second)

        left = rows[:, here] - exact_dot(rotated[...], own, last)
        rotated[:, here] = exact_dot(left, inverse[...], second)
        return carry

    lax.fori_loop(0, blocks, one_block, 0)


def rotate(rows, gram):
    columns = rows.shape[1]
    vmem = pl.BlockSpec(memory_space=pltpu.VMEM)
    return pl.pallas_call(
        rotate_kernel,
        out_shape=jax.ShapeDtypeStruct(rows.shape, jnp.float32),
        in_specs=[vmem, vmem],
        out_specs=vmem,
        scratch_shapes=[
            pltpu.VMEM((columns // LANES, LANES, columns), jnp.float32),
            pltpu.VMEM((LANES, LANES), jnp.float32),
            pltpu.VMEM((LANES, LANES), jnp.float32),
        ],
        compiler_params=pltpu.CompilerParams(vmem_limit_bytes=40 * 2**20),
        name="rotate",
    )(rows, gram)


def shards(wavefunctions, cell_ham, cell_nodes, cell_count, upper_nodes, lower_nodes):
    n_space, n_orb = lax.axis_size("space"), lax.axis_size("orb")
    current = filtered_block(
        wavefunctions[0], cell_ham[0], cell_nodes[0], cell_count[0], upper_nodes[0], lower_nodes[0], n_space
    )
    rows, gram = turn_and_gram(current, lower_nodes, n_space, n_orb)
    return rotate(rows, gram)[None]


def solution(mesh):
    in_specs = (
        P("space", None, "orb"),
        P("space", None, None, None),
        P("space", None, None),
        P("space"),
        P("space", None),
        P("space", None),
    )
    out_specs = P("space", "orb", None)
    return jax.shard_map(shards, mesh=mesh, in_specs=in_specs, out_specs=out_specs, check_vma=False)
```

profile of v0, /device:TPU:0, one launch (start us, length us, event | category | flops | bytes accessed | tf_op | source)
XLA Modules:
  0.0 156.0 jit_solution(10029044199050164190)
XLA Ops:
  0.0 7.8 %reduce-precision_convert_fusion = (bf16[4,729,729]{2,1,0:T(8,128)(2,1)S(1)}, bf16[4,729,729]{2,1,0:T(8,128)(2,1)}) fusion(f32[1,4,729,729]{3,1,2,0:T(4,128)} %param.7), kind=kLoop, calls=%fused_computation.5 | loop fusion | flops 8503056 | bytes 17006112 | tf_op jit(solution)/shard_map/convert_element_type | solution.py:196
  7.8 0.0 copy-start.2
  7.8 0.0 copy-start.3
  7.8 0.0 copy-start.1
  7.8 0.0 copy-start.4
  7.8 11.0 %fusion.2.matrices = bf16[4,1536,768]{2,1,0:T(8,128)(2,1)} fusion(bf16[4,729,729]{2,1,0:T(8,128)(2,1)} %get-tuple-element.10, bf16[4,729,729]{2,1,0:T(8,128)(2,1)S(1)} %get-tuple-element.9), kind=kLoop, calls=%fused_computation.6 | loop fusion | flops 37748736 | bytes 17940240 | tf_op jit(solution)/shard_map/concatenate | solution.py:195
  18.8 0.0 copy-done.2
  18.8 1.2 copy.7
  20.6 0.0 copy-done.3
  20.6 0.1 bitcast_select_fusion
  20.7 0.6 copy.9
  21.3 0.0 copy-done.1
  21.3 0.0 copy-done.4
  21.4 0.6 add_convert_fusion.list_row
  21.9 66.5 %filter.1.field = f32[1536,96]{1,0:T(8,128)} custom-call(f32[1536,96]{1,0:T(8,128)} %bitcast.13, bf16[4,1536,768]{2,1,0:T(8,128)(2,1)} %fusion.2.matrices, f32[1,3072]{1,0:T(1,128)} %bitcast.14, f32[1,1024]{1,0:T(1,128)} %add_convert_fusion.list_row), custom_call_target="tpu_custom_call" | custom-call | tf_op jit(solution)/shard_map/filter/pallas_call | solution.py:206
  88.4 0.0 copy-start
  88.5 1.1 copy-done
  89.6 48.2 %turn_and_gram.1 = (f32[384,384]{1,0:T(8,128)S(1)}, f32[768,128]{1,0:T(8,128)S(1)}) custom-call(f32[1536,96]{1,0:T(8,128)S(1)} %copy-done, s32[1,512]{1,0:T(1,128)S(1)} %copy-done.1), custom_call_target="tpu_custom_call" | custom-call | tf_op jit(solution)/shard_map/turn_and_gram/pallas_call | solution.py:337
  137.8 18.2 %rotate.1 = f32[384,384]{1,0:T(8,128)} custom-call(f32[384,384]{1,0:T(8,128)S(1)} %get-tuple-element.7.rows, f32[768,128]{1,0:T(8,128)S(1)} %get-tuple-element.8.gram), custom_call_target="tpu_custom_call" | custom-call | tf_op jit(solution)/shard_map/rotate/pallas_call | solution.py:444
  (2 shorter events, 0.0 us)
Async XLA Ops:
  7.8 11.0 %copy-start.2 = (f32[1,1536,96]{1,2,0:T(8,128)S(1)}, f32[1,1536,96]{1,2,0:T(8,128)}, u32[]{:S(2)}) copy-start(f32[1,1536,96]{1,2,0:T(8,128)} %param.6) | copy-start | bytes 1769476
  7.8 12.8 %copy-start.3 = (s32[1,4,729]{2,1,0:T(4,128)S(1)}, s32[1,4,729]{2,1,0:T(4,128)}, u32[]{:S(2)}) copy-start(s32[1,4,729]{2,1,0:T(4,128)} %param.8) | copy-start | bytes 34996
  7.8 13.5 %copy-start.1 = (s32[1,512]{1,0:T(1,128)S(1)}, s32[1,512]{1,0:T(1,128)}, u32[]{:S(2)}) copy-start(s32[1,512]{1,0:T(1,128)} %lower_list.1) | copy-start | bytes 6148
  7.8 13.5 %copy-start.4 = (s32[1,512]{1,0:T(1,128)S(1)}, s32[1,512]{1,0:T(1,128)}, u32[]{:S(2)}) copy-start(s32[1,512]{1,0:T(1,128)} %param.10) | copy-start | bytes 6148
  88.4 1.1 copy-start
where the time goes:
time: 156 us
  Pallas kernels  133 us (85%)
  other arithmetic  19.5 us (12%)
  local copies, waits for them, and re-layouts  2.91 us (2%)
    pallas_call x1, Pallas kernels, filtered_block(): pl.pallas_call(functools.partial(filter_kernel, n_space, DEGREE), out_sha...  66.5 us
    pallas_call x1, Pallas kernels, turn_and_gram(): pl.pallas_call(functools.partial(gram_kernel, n_space, n_orb, inside), ou...  48.2 us
    pallas_call x1, Pallas kernels, rotate(): pl.pallas_call(rotate_kernel, out_shape=jax.ShapeDtypeStruct(rows.shape,...  18.2 us
    concatenate x1, other arithmetic, filtered_block(): jnp.concatenate([jnp.pad(piece.astype(jnp.bfloat16), margin) for piece in...  11 us
    convert_element_type x1, other arithmetic, filtered_block(): piece.astype(jnp.bfloat16)  7.81 us

commit v1 on v0

--- a/solution.py
+++ b/solution.py
@@ -30,7 +30,34 @@
     return product[:, :LANES] + product[:, LANES:]
 
 
-def filter_kernel(n_space, degree, start, matrices, node_row, list_row, out, gather, scatter, pick, place, stack,
+def dense_rows(count, width):
+    return count * width // LANES if 4 * width == 3 * LANES and count % 32 == 0 else count
+
+
+def dense(values, width):
+    count = values.shape[0]
+    if dense_rows(count, width) == count:
+        return values
+    rest, side = count // 4, LANES - width
+    tail = values[count - rest :, :]
+    beside = [tail[:, at : at + side] for at in range(0, width, side)]
+    return jnp.concatenate([values[: count - rest, :width], jnp.concatenate(beside, axis=0)], axis=1)
+
+
+def sparse(values, count, width):
+    if dense_rows(count, width) == count:
+        return values[:, :width]
+    rest = count // 4
+    beside = [values[at : at + rest, width:] for at in range(0, count - rest, rest)]
+    return jnp.concatenate([values[:, :width], jnp.concatenate(beside, axis=1)], axis=0)
+
+
+def widened(values):
+    room = LANES - values.shape[1]
+    return jnp.concatenate([values, jnp.zeros((values.shape[0], room), values.dtype)], axis=1) if room else values
+
+
+def filter_kernel(n_space, n_orb, degree, start, matrices, node_row, list_row, out, gather, scatter, pick, place, stack, raw,
                   fields, packed, cell_out, sums, outgoing, arriving, load_sem, send_sem, recv_sem):
     space = lax.axis_index("space")
     nodes, width = start.shape
@@ -38,8 +65,11 @@
     slots = list_row.shape[1] // 2
     has_above, has_below = space < n_space - 1, space > 0
 
-    for cell in range(cells):
-        pltpu.make_async_copy(matrices.at[cell], stack.at[cell], load_sem.at[cell]).start()
+    def load(cell):
+        return pltpu.make_async_copy(matrices.at[cell], raw.at[cell % 2], load_sem.at[cell])
+
+    for cell in range(min(cells, 2)):
+        load(cell).start()
     arriving[...] = jnp.zeros_like(arriving)
 
     barrier = pltpu.get_barrier_semaphore()
@@ -89,7 +119,7 @@
             there = slice(tile * LANES, (tile + 1) * LANES)
             other = (tile * LANES + slots) % (2 * slots)
             place[here, there] = ones_where(node == list_row[:, other : other + LANES])
-        values = jnp.concatenate([start[here, :], jnp.zeros((LANES, LANES - width), jnp.float32)], axis=1)
+        values = widened(start[here, :])
         fields[0, here, :] = values
         fields[1, here, :] = values
         high, low = split(values)
@@ -98,10 +128,23 @@
         return carry
 
     lax.fori_loop(0, node_row.shape[1] // LANES, gather_rows, 0)
-    lax.fori_loop(0, 2 * slots // LANES, pick_rows, 0)
-    lax.fori_loop(0, nodes // LANES, node_rows, 0)
     for cell in range(cells):
-        pltpu.make_async_copy(matrices.at[cell], stack.at[cell], load_sem.at[cell]).wait()
+        load(cell).wait()
+
+        def split_rows(chunk, carry):
+            here = tile_at(chunk)
+            high, low = split(raw[cell % 2, here, :])
+            stack[cell, here, :] = high
+            stack[cell, pl.ds(pl.multiple_of(cell_size + chunk * LANES, LANES), LANES), :] = low
+            return carry
+
+        lax.fori_loop(0, cell_size // LANES, split_rows, 0)
+        if cell + 2 < cells:
+            load(cell + 2).start()
+        if cell == 0:
+            lax.fori_loop(0, 2 * slots // LANES, pick_rows, 0)
+        if cell == min(cells - 1, 1):
+            lax.fori_loop(0, nodes // LANES, node_rows, 0)
     pl.semaphore_wait(barrier, has_above.astype(jnp.int32) + has_below.astype(jnp.int32))
 
     part = nodes // 3 if nodes % (3 * LANES) == 0 else LANES
@@ -130,13 +173,13 @@
             )
 
         down, up = transfer(0, space - 1), transfer(1, space + 1)
-        outgoing[0] = folded(plain_dot(pick[:slots, :], cell_out[...]))
+        outgoing[0] = dense(folded(plain_dot(pick[:slots, :], cell_out[...])), width)
 
         @pl.when(has_below)
         def _():
             down.start()
 
-        outgoing[1] = folded(plain_dot(pick[slots:, :], cell_out[...]))
+        outgoing[1] = dense(folded(plain_dot(pick[slots:, :], cell_out[...])), width)
 
         @pl.when(has_above)
         def _():
@@ -163,7 +206,7 @@
         first = step == 0
         scale = jnp.where(first, 1.0 / half_width, 2.0 / half_width)
         keep = jnp.where(first, 0.0, 1.0)
-        parts = [split(arriving[step, way]) for way in range(2)]
+        parts = [split(widened(sparse(arriving[step, way], slots, width))) for way in range(2)]
         arrived = jnp.concatenate([jnp.concatenate(pair, axis=1) for pair in parts], axis=0)
 
         def advance(chunk, carry):
@@ -180,32 +223,33 @@
         return carry
 
     lax.fori_loop(0, degree, apply, 0)
-    out[...] = fields[degree % 2, :, :width]
-
-
-def filtered_block(start, matrices, node_map, live_cells, upper_list, lower_list, n_space):
+    quarter = nodes // n_orb
+    for which in range(n_orb):
+        out[which] = dense(fields[degree % 2, which * quarter : (which + 1) * quarter, :width], width)
+
+
+def filtered_block(start, matrices, node_map, live_cells, upper_list, lower_list, n_space, n_orb):
     nodes, width = start.shape
     cells, cell_nodes = node_map.shape
     cell_size = -(-cell_nodes // LANES) * LANES
     room = cell_size - cell_nodes
     slots = upper_list.shape[0]
 
-    high = lax.reduce_precision(matrices, exponent_bits=8, mantissa_bits=7)
-    margin = ((0, 0), (0, room), (0, room))
-    stack = jnp.concatenate(
-        [jnp.pad(piece.astype(jnp.bfloat16), margin) for piece in (high, matrices - high)], axis=1
-    )
+    padded = jnp.pad(matrices, ((0, 0), (0, room), (0, room)))
     live = jnp.arange(cells)[:, None] < live_cells
     node_row = jnp.pad(jnp.where(live, node_map, -1), ((0, 0), (0, room)), constant_values=-1)
     node_row = node_row.reshape(1, cells * cell_size).astype(jnp.float32)
     list_row = jnp.concatenate([lower_list, upper_list]).reshape(1, 2 * slots).astype(jnp.float32)
 
+    sent = dense_rows(nodes // n_orb, width)
+    packed_width = LANES if sent != nodes // n_orb else width
+    slot_rows = dense_rows(slots, width)
     vmem, anywhere = pl.BlockSpec(memory_space=pltpu.VMEM), pl.BlockSpec(memory_space=pl.ANY)
     dma = pltpu.SemaphoreType.DMA
     every, half = jnp.float32, jnp.bfloat16
     return pl.pallas_call(
-        functools.partial(filter_kernel, n_space, DEGREE),
-        out_shape=jax.ShapeDtypeStruct(start.shape, jnp.float32),
+        functools.partial(filter_kernel, n_space, n_orb, DEGREE),
+        out_shape=jax.ShapeDtypeStruct((n_orb, sent, packed_width), jnp.float32),
         in_specs=[vmem, anywhere, vmem, vmem],
         out_specs=vmem,
         scratch_shapes=[
@@ -214,12 +258,13 @@
             pltpu.VMEM((2 * slots, cells * cell_size), half),
             pltpu.VMEM((nodes, 2 * slots), half),
             pltpu.VMEM((cells, 2 * cell_size, cell_size), half),
+            pltpu.VMEM((2, cell_size, cell_size), every),
             pltpu.VMEM((2, nodes, LANES), every),
             pltpu.VMEM((nodes, 2 * LANES), half),
             pltpu.VMEM((cells * cell_size, 2 * LANES), half),
             pltpu.VMEM((nodes, LANES), every),
-            pltpu.VMEM((2, slots, LANES), every),
-            pltpu.VMEM((DEGREE, 2, slots, LANES), every),
+            pltpu.VMEM((2, slot_rows, LANES), every),
+            pltpu.VMEM((DEGREE, 2, slot_rows, LANES), every),
             dma((cells,)),
             dma((DEGREE, 2)),
             dma((DEGREE, 2)),
@@ -228,7 +273,7 @@
             collective_id=2, has_side_effects=True, vmem_limit_bytes=58 * 2**20
         ),
         name="filter",
-    )(start, stack, node_row, list_row)
+    )(start, padded, node_row, list_row)
 
 
 def exact_dot(left, right, dims):
@@ -245,12 +290,11 @@
     return [(i, j) for i in range(blocks) for j in range(i + 1)]
 
 
-def gram_kernel(n_space, n_orb, inside, field, lower_list, rows_out, gram_out, pieces, local, parts, slab, others,
+def gram_kernel(n_space, n_orb, node_total, inside, field, lower_list, rows_out, gram_out, pieces, local, parts, slab, others,
                 turn_send, turn_recv, split_send, split_recv, orb_send, orb_recv, join_send, join_recv):
     space, orb = lax.axis_index("space"), lax.axis_index("orb")
-    node_total, width = field.shape
-    quarter = node_total // n_orb
-    columns = width * n_orb
+    quarter, columns = rows_out.shape
+    width = columns // n_orb
     partners = n_orb - 1
 
     barrier = pltpu.get_barrier_semaphore()
@@ -278,18 +322,15 @@
             copies.append(copy)
         return copies
 
-    def own_quarter(which):
-        return field.at[pl.ds(pl.multiple_of(which * quarter, 8), quarter)]
-
-    copies = exchange("orb", n_orb, orb, turn_send, turn_recv, own_quarter, pieces.at[orb])
-    pieces[orb] = field[pl.ds(pl.multiple_of(orb * quarter, 8), quarter), :]
+    copies = exchange("orb", n_orb, orb, turn_send, turn_recv, lambda other: field.at[other], pieces.at[orb])
+    pieces[orb] = field[orb]
     node = lax.broadcasted_iota(jnp.int32, (quarter, lower_list.shape[1]), 0) + orb * quarter
     hits = jnp.where(node == lower_list[...], 1.0, 0.0)
     weight = (1.0 - jnp.max(hits, axis=1, keepdims=True)) * (1.0 / (n_space * node_total))
     for copy in copies:
         copy.wait()
     for which in range(n_orb):
-        rows_out[:, which * width : (which + 1) * width] = pieces[which]
+        rows_out[:, which * width : (which + 1) * width] = sparse(pieces[which], quarter, width)
 
     blocks = columns // LANES
     for spot, (i, j) in enumerate(block_pairs(blocks)):
@@ -325,8 +366,7 @@
         copy.wait()
 
 
-def turn_and_gram(field, lower_list, n_space, n_orb):
-    node_total, width = field.shape
+def turn_and_gram(field, lower_list, node_total, width, n_space, n_orb):
     quarter, columns = node_total // n_orb, width * n_orb
     packed = len(block_pairs(columns // LANES)) * LANES
     inside = n_space <= 8 and packed % (8 * n_space) == 0
@@ -335,7 +375,7 @@
     dma = pltpu.SemaphoreType.DMA
     vmem = pl.BlockSpec(memory_space=pltpu.VMEM)
     rows, gram = pl.pallas_call(
-        functools.partial(gram_kernel, n_space, n_orb, inside),
+        functools.partial(gram_kernel, n_space, n_orb, node_total, inside),
         out_shape=(
             jax.ShapeDtypeStruct((quarter, columns), jnp.float32),
             jax.ShapeDtypeStruct((packed, LANES), jnp.float32),
@@ -343,7 +383,7 @@
         in_specs=[vmem, vmem],
         out_specs=(vmem, vmem),
         scratch_shapes=[
-            pltpu.VMEM((n_orb, quarter, width), jnp.float32),
+            pltpu.VMEM(field.shape, jnp.float32),
             pltpu.VMEM((packed, LANES), jnp.float32),
             pltpu.VMEM((groups, chunk, LANES), jnp.float32),
             pltpu.VMEM((chunk, LANES), jnp.float32),
@@ -459,9 +499,10 @@
 def shards(wavefunctions, cell_ham, cell_nodes, cell_count, upper_nodes, lower_nodes):
     n_space, n_orb = lax.axis_size("space"), lax.axis_size("orb")
     current = filtered_block(
-        wavefunctions[0], cell_ham[0], cell_nodes[0], cell_count[0], upper_nodes[0], lower_nodes[0], n_space
+        wavefunctions[0], cell_ham[0], cell_nodes[0], cell_count[0], upper_nodes[0], lower_nodes[0],
+        n_space, n_orb,
     )
-    rows, gram = turn_and_gram(current, lower_nodes, n_space, n_orb)
+    rows, gram = turn_and_gram(current, lower_nodes, *wavefunctions.shape[1:], n_space, n_orb)
     return rotate(rows, gram)[None]
 
 

time: 156 us -> 143 us (0.917)
  other arithmetic: 19.5 us -> 0.68 us
  local copies, waits for them, and re-layouts: 2.91 us -> 12.7 us
  Pallas kernels: 133 us -> 128 us
    concatenate x1 -> x0, other arithmetic: 11 us -> none  [filtered_block(): jnp.concatenate([jnp.pad(piece.astype(jnp.bfloat16), margin) for piece in...]
    convert_element_type x1 -> x0, other arithmetic: 7.81 us -> none  [filtered_block(): piece.astype(jnp.bfloat16)]
    unnamed x12 -> x13, local copies, waits for them, and re-layouts: 2.91 us -> 8.12 us
    pallas_call x2, Pallas kernels: 115 us -> 110 us  [the longest x1 68.1 us: filtered_block(): pl.pallas_call(functools.partial(filter_kernel, n_space, n_orb, DEGREE),...]
    pad x0 -> x1, local copies, waits for them, and re-layouts: none -> 4.6 us  [filtered_block(): padded = jnp.pad(matrices, ((0, 0), (0, room), (0, room)))]
where the time goes in v1:
time: 143 us; the launch traced here: 142 us
  Pallas kernels  128 us (90%)
  local copies, waits for them, and re-layouts  12.7 us (9%)
    pallas_call x1, Pallas kernels, filtered_block(): pl.pallas_call(functools.partial(filter_kernel, n_space, n_orb, DEGREE),...  68.1 us
    pallas_call x1, Pallas kernels, turn_and_gram(): pl.pallas_call(functools.partial(gram_kernel, n_space, n_orb, node_total,...  41.7 us
    pallas_call x1, Pallas kernels, rotate(): pl.pallas_call(rotate_kernel, out_shape=jax.ShapeDtypeStruct(rows.shape,...  18.4 us
    unnamed x13, local copies, waits for them, and re-layouts  8.12 us
    pad x1, local copies, waits for them, and re-layouts, filtered_block(): padded = jnp.pad(matrices, ((0, 0), (0, room), (0, room)))  4.6 us

profile of v1, /device:TPU:0, one launch (start us, length us, event | category | flops | bytes accessed | tf_op | source)
XLA Modules:
  0.0 142.3 jit_solution(8635256407804751513)
XLA Ops:
  0.0 5.3 %copy.11 = f32[1,4,729,729]{3,2,1,0:T(8,128)S(1)} copy(f32[1,4,729,729]{3,1,2,0:T(4,128)} %param.7) | data formatting | bytes 17006112 | tf_op args[1]
  5.3 0.0 copy-start.2
  5.3 0.0 copy-start.3
  5.3 0.0 copy-start.1
  5.3 0.0 copy-start.4
  5.3 4.6 %pad.8.matrices = f32[4,768,768]{2,1,0:T(8,128)} pad(f32[4,729,729]{2,1,0:T(8,128)S(1)} %bitcast.13, f32[]{:T(128)} %constant.1.clone.1), padding=0_0x0_39x0_39 | pad | bytes 17940244 | tf_op jit(solution)/shard_map/jit(_pad)/pad | solution.py:238
  9.9 0.0 copy-done.2
  9.9 1.1 copy.7
  11.7 0.0 copy-done.3
  11.7 0.1 bitcast_select_fusion
  11.8 0.6 copy.9
  12.4 0.0 copy-done.1
  12.4 0.0 copy-done.4
  12.4 0.6 add_convert_fusion.list_row
  13.0 68.1 %filter.1.field = f32[4,288,128]{2,1,0:T(8,128)} custom-call(f32[1536,96]{1,0:T(8,128)} %bitcast.14, f32[4,768,768]{2,1,0:T(8,128)} %pad.8.matrices, f32[1,3072]{1,0:T(1,128)} %bitcast.15, f32[1,1024]{1,0:T(1,128)} %add_convert_fusion.list_row), custom_call_target="tpu_custom_call" | custom-call | tf_op jit(solution)/shard_map/filter/pallas_call | solution.py:250
  81.2 0.0 copy-start
  81.2 1.1 copy-done
  82.2 41.7 %turn_and_gram.1 = (f32[384,384]{1,0:T(8,128)S(1)}, f32[768,128]{1,0:T(8,128)S(1)}) custom-call(f32[4,288,128]{2,1,0:T(8,128)S(1)} %copy-done, s32[1,512]{1,0:T(1,128)S(1)} %copy-done.1), custom_call_target="tpu_custom_call" | custom-call | tf_op jit(solution)/shard_map/turn_and_gram/pallas_call | solution.py:377
  123.9 18.4 %rotate.1 = f32[384,384]{1,0:T(8,128)} custom-call(f32[384,384]{1,0:T(8,128)S(1)} %get-tuple-element.7.rows, f32[768,128]{1,0:T(8,128)S(1)} %get-tuple-element.8.gram), custom_call_target="tpu_custom_call" | custom-call | tf_op jit(solution)/shard_map/rotate/pallas_call | solution.py:484
  (2 shorter events, 0.0 us)
Async XLA Ops:
  5.3 4.6 %copy-start.2 = (f32[1,1536,96]{1,2,0:T(8,128)S(1)}, f32[1,1536,96]{1,2,0:T(8,128)}, u32[]{:S(2)}) copy-start(f32[1,1536,96]{1,2,0:T(8,128)} %param.6) | copy-start | bytes 1769476
  5.3 6.4 %copy-start.3 = (s32[1,4,729]{2,1,0:T(4,128)S(1)}, s32[1,4,729]{2,1,0:T(4,128)}, u32[]{:S(2)}) copy-start(s32[1,4,729]{2,1,0:T(4,128)} %param.8) | copy-start | bytes 34996
  5.3 7.1 %copy-start.1 = (s32[1,512]{1,0:T(1,128)S(1)}, s32[1,512]{1,0:T(1,128)}, u32[]{:S(2)}) copy-start(s32[1,512]{1,0:T(1,128)} %lower_list.1) | copy-start | bytes 6148
  5.3 7.1 %copy-start.4 = (s32[1,512]{1,0:T(1,128)S(1)}, s32[1,512]{1,0:T(1,128)}, u32[]{:S(2)}) copy-start(s32[1,512]{1,0:T(1,128)} %param.10) | copy-start | bytes 6148
  81.2 1.1 copy-start

commit v2 on v1

--- a/solution.py
+++ b/solution.py
@@ -60,8 +60,11 @@
 def filter_kernel(n_space, n_orb, degree, start, matrices, node_row, list_row, out, gather, scatter, pick, place, stack, raw,
                   fields, packed, cell_out, sums, outgoing, arriving, load_sem, send_sem, recv_sem):
     space = lax.axis_index("space")
-    nodes, width = start.shape
+    width, nodes = start.shape
     cells, doubled, cell_size = stack.shape
+    cell_nodes = raw.shape[1]
+    whole = cell_nodes // 8 * 8
+    tail_at = whole // 16 * 16
     slots = list_row.shape[1] // 2
     has_above, has_below = space < n_space - 1, space > 0
 
@@ -119,7 +122,10 @@
             there = slice(tile * LANES, (tile + 1) * LANES)
             other = (tile * LANES + slots) % (2 * slots)
             place[here, there] = ones_where(node == list_row[:, other : other + LANES])
-        values = widened(start[here, :])
+        block = start[:, here]
+        if width < LANES:
+            block = jnp.concatenate([block, jnp.zeros((LANES - width, LANES), jnp.float32)], axis=0)
+        values = jnp.transpose(block)
         fields[0, here, :] = values
         fields[1, here, :] = values
         high, low = split(values)
@@ -131,14 +137,36 @@
     for cell in range(cells):
         load(cell).wait()
 
+        def put_split(at, values):
+            high, low = split(values)
+            stack[cell, pl.ds(at, values.shape[0]), :] = high
+            stack[cell, pl.ds(cell_size + at, values.shape[0]), :] = low
+
+        def widen(values):
+            room = cell_size - cell_nodes
+            return jnp.concatenate([values, jnp.zeros((values.shape[0], room), jnp.float32)], axis=1)
+
         def split_rows(chunk, carry):
-            here = tile_at(chunk)
-            high, low = split(raw[cell % 2, here, :])
-            stack[cell, here, :] = high
-            stack[cell, pl.ds(pl.multiple_of(cell_size + chunk * LANES, LANES), LANES), :] = low
+            put_split(pl.multiple_of(chunk * LANES, LANES), widen(raw[cell % 2, tile_at(chunk), :]))
             return carry
 
-        lax.fori_loop(0, cell_size // LANES, split_rows, 0)
+        lax.fori_loop(0, tail_at // LANES, split_rows, 0)
+        done = tail_at // LANES * LANES
+        if tail_at > done:
+            put_split(done, widen(raw[cell % 2, done:tail_at, :]))
+        if cell_size > tail_at:
+            pieces = [widen(raw[cell % 2, tail_at:whole, :])] if whole > tail_at else []
+            if cell_nodes > whole:
+                row_id = lax.broadcasted_iota(jnp.int32, (8, cell_size), 0)
+                block = jnp.zeros((8, cell_size), jnp.float32)
+                for row in range(whole, cell_nodes):
+                    value = jnp.broadcast_to(widen(raw[cell % 2, row : row + 1, :]), (8, cell_size))
+                    block = jnp.where(row_id == row - whole, value, block)
+                pieces.append(block)
+            room = cell_size - tail_at - sum(piece.shape[0] for piece in pieces)
+            if room:
+                pieces.append(jnp.zeros((room, cell_size), jnp.float32))
+            put_split(tail_at, jnp.concatenate(pieces, axis=0))
         if cell + 2 < cells:
             load(cell + 2).start()
         if cell == 0:
@@ -235,7 +263,6 @@
     room = cell_size - cell_nodes
     slots = upper_list.shape[0]
 
-    padded = jnp.pad(matrices, ((0, 0), (0, room), (0, room)))
     live = jnp.arange(cells)[:, None] < live_cells
     node_row = jnp.pad(jnp.where(live, node_map, -1), ((0, 0), (0, room)), constant_values=-1)
     node_row = node_row.reshape(1, cells * cell_size).astype(jnp.float32)
@@ -258,7 +285,7 @@
             pltpu.VMEM((2 * slots, cells * cell_size), half),
             pltpu.VMEM((nodes, 2 * slots), half),
             pltpu.VMEM((cells, 2 * cell_size, cell_size), half),
-            pltpu.VMEM((2, cell_size, cell_size), every),
+            pltpu.VMEM((2, cell_nodes, cell_nodes), every),
             pltpu.VMEM((2, nodes, LANES), every),
             pltpu.VMEM((nodes, 2 * LANES), half),
             pltpu.VMEM((cells * cell_size, 2 * LANES), half),
@@ -273,7 +300,7 @@
             collective_id=2, has_side_effects=True, vmem_limit_bytes=58 * 2**20
         ),
         name="filter",
-    )(start, padded, node_row, list_row)
+    )(jnp.swapaxes(start, 0, 1), matrices, node_row, list_row)
 
 
 def exact_dot(left, right, dims):
@@ -448,34 +475,42 @@
         inverse[below:, :] = rest_eye
 
 
+def parts_dot(left, right):
+    dims = (((1,), (1,)), ((), ()))
+    (left_high, left_low), (right_high, right_low) = split(left), split(right)
+
+    def product(a, b):
+        return lax.dot_general(a, b, dims, preferred_element_type=jnp.float32)
+
+    return product(left_high, right_high) + (product(left_high, right_low) + product(left_low, right_high))
+
+
 def rotate_kernel(rows, gram, rotated, lower, block, inverse):
-    columns = rows.shape[1]
-    blocks = columns // LANES
-    lower[...] = jnp.zeros_like(lower)
-    rotated[...] = jnp.zeros_like(rotated)
-    last, second = ((1,), (1,)), ((1,), (1,))
-
-    def one_block(k, carry):
-        here = pl.ds(pl.multiple_of(k * LANES, LANES), LANES)
-        spot = (k * (k + 3)) // 2
-        own = lower[k]
-        diagonal = gram[pl.ds(pl.multiple_of(spot * LANES, LANES), LANES), :]
-        block[...] = diagonal - exact_dot(own, own, last)
-        invert_factor(block, inverse)
-        for i in range(1, blocks):
-
-            @pl.when(i > k)
-            def _():
-                at = (i * (i + 1)) // 2 + k
-                under = gram[pl.ds(pl.multiple_of(at * LANES, LANES), LANES), :]
-                under = under - exact_dot(lower[i], own, last)
-                lower[i, :, here] = exact_dot(under, inverse[...], second)
-
-        left = rows[:, here] - exact_dot(rotated[...], own, last)
-        rotated[:, here] = exact_dot(left, inverse[...], second)
-        return carry
-
-    lax.fori_loop(0, blocks, one_block, 0)
+    blocks = rows.shape[1] // LANES
+    last = ((1,), (1,))
+
+    def span(k):
+        return slice(k * LANES, (k + 1) * LANES)
+
+    for k in range(blocks):
+        before = slice(0, k * LANES)
+        spot = k * (k + 3) // 2
+        diagonal = gram[span(spot), :]
+        if k:
+            own = lower[k, :, before]
+            diagonal = diagonal - exact_dot(own, own, last)
+        block[k] = diagonal
+        invert_factor(block.at[k], inverse.at[k])
+        solved = inverse[k]
+        for i in range(k + 1, blocks):
+            under = gram[span(i * (i + 1) // 2 + k), :]
+            if k:
+                under = under - exact_dot(lower[i, :, before], own, last)
+            lower[i, :, span(k)] = exact_dot(under, solved, last)
+        left = rows[:, span(k)]
+        if k:
+            left = left - parts_dot(rotated[:, before], own)
+        rotated[:, span(k)] = parts_dot(left, solved)
 
 
 def rotate(rows, gram):
@@ -488,8 +523,8 @@
         out_specs=vmem,
         scratch_shapes=[
             pltpu.VMEM((columns // LANES, LANES, columns), jnp.float32),
-            pltpu.VMEM((LANES, LANES), jnp.float32),
-            pltpu.VMEM((LANES, LANES), jnp.float32),
+            pltpu.VMEM((columns // LANES, LANES, LANES), jnp.float32),
+            pltpu.VMEM((columns // LANES, LANES, LANES), jnp.float32),
         ],
         compiler_params=pltpu.CompilerParams(vmem_limit_bytes=40 * 2**20),
         name="rotate",

time: 143 us -> 137 us (0.958)
  Pallas kernels: 128 us -> 123 us
  local copies, waits for them, and re-layouts: 12.7 us -> 10.4 us
    pallas_call x1, Pallas kernels: 18.4 us -> 12.8 us  [rotate(): pl.pallas_call(rotate_kernel, out_shape=jax.ShapeDtypeStruct(rows.shape,...]
    pad x1 -> x0, local copies, waits for them, and re-layouts: 4.6 us -> none  [filtered_block(): padded = jnp.pad(matrices, ((0, 0), (0, room), (0, room)))]
    unnamed x13 -> x6, local copies, waits for them, and re-layouts: 8.12 us -> 10.4 us
where the time goes in v2:
time: 137 us
  Pallas kernels  123 us (90%)
  local copies, waits for them, and re-layouts  10.4 us (8%)
  other arithmetic  2.08 us (2%)
    pallas_call x1, Pallas kernels, filtered_block(): pl.pallas_call(functools.partial(filter_kernel, n_space, n_orb, DEGREE),...  68.9 us
    pallas_call x1, Pallas kernels, turn_and_gram(): pl.pallas_call(functools.partial(gram_kernel, n_space, n_orb, node_total,...  41.7 us
    pallas_call x1, Pallas kernels, rotate(): pl.pallas_call(rotate_kernel, out_shape=jax.ShapeDtypeStruct(rows.shape,...  12.8 us
    unnamed x6, local copies, waits for them, and re-layouts  10.4 us

profile of v2, /device:TPU:0, one launch (start us, length us, event | category | flops | bytes accessed | tf_op | source)
XLA Modules:
  0.0 136.5 jit_solution(878022915443670373)
XLA Ops:
  0.7 1.3 add_convert_fusion.list_row
  1.9 0.8 bitcast_select_fusion
  2.7 0.6 copy.8
  3.4 8.8 %copy.10 = f32[1,4,729,729]{3,2,1,0:T(8,128)} copy(f32[1,4,729,729]{3,1,2,0:T(4,128)} %param.7) | data formatting | bytes 17006112 | tf_op args[1]
  12.1 0.0 copy-start.1
  12.1 68.9 %filter.1.field = f32[4,288,128]{2,1,0:T(8,128)} custom-call(f32[96,1536]{1,0:T(8,128)} %bitcast.16, f32[4,729,729]{2,1,0:T(8,128)} %bitcast.15, f32[1,3072]{1,0:T(1,128)} %bitcast.17, f32[1,1024]{1,0:T(1,128)} %add_convert_fusion.list_row), custom_call_target="tpu_custom_call" | custom-call | tf_op jit(solution)/shard_map/filter/pallas_call | solution.py:277
  81.0 0.0 copy-done.1
  81.0 0.0 copy-start
  81.0 1.1 copy-done
  82.1 41.7 %turn_and_gram.1 = (f32[384,384]{1,0:T(8,128)S(1)}, f32[768,128]{1,0:T(8,128)S(1)}) custom-call(f32[4,288,128]{2,1,0:T(8,128)S(1)} %copy-done, s32[1,512]{1,0:T(1,128)S(1)} %copy-done.1), custom_call_target="tpu_custom_call" | custom-call | tf_op jit(solution)/shard_map/turn_and_gram/pallas_call | solution.py:404
  123.7 12.8 %rotate.1 = f32[384,384]{1,0:T(8,128)} custom-call(f32[384,384]{1,0:T(8,128)S(1)} %get-tuple-element.7.rows, f32[768,128]{1,0:T(8,128)S(1)} %get-tuple-element.8.gram), custom_call_target="tpu_custom_call" | custom-call | tf_op jit(solution)/shard_map/rotate/pallas_call | solution.py:519
  (2 shorter events, 0.0 us)
Async XLA Ops:
  12.1 68.9 %copy-start.1 = (s32[1,512]{1,0:T(1,128)S(1)}, s32[1,512]{1,0:T(1,128)}, u32[]{:S(2)}) copy-start(s32[1,512]{1,0:T(1,128)} %lower_list.1) | copy-start | bytes 6148
  81.0 1.1 copy-start

commit v3 on v2

--- a/solution.py
+++ b/solution.py
@@ -57,7 +57,7 @@
     return jnp.concatenate([values, jnp.zeros((values.shape[0], room), values.dtype)], axis=1) if room else values
 
 
-def filter_kernel(n_space, n_orb, degree, start, matrices, node_row, list_row, out, gather, scatter, pick, place, stack, raw,
+def filter_kernel(n_space, n_orb, degree, start, matrices, node_map, live, lower_list, upper_list, out, gather, scatter, pick, place, stack, raw, node_row, list_row,
                   fields, packed, cell_out, sums, outgoing, arriving, load_sem, send_sem, recv_sem):
     space = lax.axis_index("space")
     width, nodes = start.shape
@@ -66,6 +66,15 @@
     whole = cell_nodes // 8 * 8
     tail_at = whole // 16 * 16
     slots = list_row.shape[1] // 2
+    list_row[:, :slots] = lower_list[...].astype(jnp.float32)
+    list_row[:, slots:] = upper_list[...].astype(jnp.float32)
+    count = live[...].astype(jnp.float32)
+    for cell in range(cells):
+        row = jnp.where(count > float(cell), node_map[cell : cell + 1, :].astype(jnp.float32), -1.0)
+        room = cell_size - row.shape[1]
+        if room:
+            row = jnp.concatenate([row, jnp.full((1, room), -1.0, jnp.float32)], axis=1)
+        node_row[:, cell * cell_size : (cell + 1) * cell_size] = row
     has_above, has_below = space < n_space - 1, space > 0
 
     def load(cell):
@@ -260,13 +269,7 @@
     nodes, width = start.shape
     cells, cell_nodes = node_map.shape
     cell_size = -(-cell_nodes // LANES) * LANES
-    room = cell_size - cell_nodes
-    slots = upper_list.shape[0]
-
-    live = jnp.arange(cells)[:, None] < live_cells
-    node_row = jnp.pad(jnp.where(live, node_map, -1), ((0, 0), (0, room)), constant_values=-1)
-    node_row = node_row.reshape(1, cells * cell_size).astype(jnp.float32)
-    list_row = jnp.concatenate([lower_list, upper_list]).reshape(1, 2 * slots).astype(jnp.float32)
+    slots = upper_list.shape[1]
 
     sent = dense_rows(nodes // n_orb, width)
     packed_width = LANES if sent != nodes // n_orb else width
@@ -277,7 +280,7 @@
     return pl.pallas_call(
         functools.partial(filter_kernel, n_space, n_orb, DEGREE),
         out_shape=jax.ShapeDtypeStruct((n_orb, sent, packed_width), jnp.float32),
-        in_specs=[vmem, anywhere, vmem, vmem],
+        in_specs=[vmem, anywhere, vmem, vmem, vmem, vmem],
         out_specs=vmem,
         scratch_shapes=[
             pltpu.VMEM((cells * cell_size, nodes), half),
@@ -286,6 +289,8 @@
             pltpu.VMEM((nodes, 2 * slots), half),
             pltpu.VMEM((cells, 2 * cell_size, cell_size), half),
             pltpu.VMEM((2, cell_nodes, cell_nodes), every),
+            pltpu.VMEM((1, cells * cell_size), every),
+            pltpu.VMEM((1, 2 * slots), every),
             pltpu.VMEM((2, nodes, LANES), every),
             pltpu.VMEM((nodes, 2 * LANES), half),
             pltpu.VMEM((cells * cell_size, 2 * LANES), half),
@@ -300,7 +305,7 @@
             collective_id=2, has_side_effects=True, vmem_limit_bytes=58 * 2**20
         ),
         name="filter",
-    )(jnp.swapaxes(start, 0, 1), matrices, node_row, list_row)
+    )(jnp.swapaxes(start, 0, 1), matrices, node_map, live_cells, lower_list, upper_list)
 
 
 def exact_dot(left, right, dims):
@@ -534,7 +539,7 @@
 def shards(wavefunctions, cell_ham, cell_nodes, cell_count, upper_nodes, lower_nodes):
     n_space, n_orb = lax.axis_size("space"), lax.axis_size("orb")
     current = filtered_block(
-        wavefunctions[0], cell_ham[0], cell_nodes[0], cell_count[0], upper_nodes[0], lower_nodes[0],
+        wavefunctions[0], cell_ham[0], cell_nodes[0], cell_count[:, None], upper_nodes, lower_nodes,
         n_space, n_orb,
     )
     rows, gram = turn_and_gram(current, lower_nodes, *wavefunctions.shape[1:], n_space, n_orb)

time: 137 us -> 134 us (0.978)
  other arithmetic: 2.08 us -> 0 us
    unnamed x6 -> x5, local copies, waits for them, and re-layouts: 10.4 us -> 9.82 us
where the time goes in v3:
time: 134 us
  Pallas kernels  123 us (92%)
  local copies, waits for them, and re-layouts  9.82 us (7%)
    pallas_call x1, Pallas kernels, filtered_block(): pl.pallas_call(functools.partial(filter_kernel, n_space, n_orb, DEGREE),...  68.9 us
    pallas_call x1, Pallas kernels, turn_and_gram(): pl.pallas_call(functools.partial(gram_kernel, n_space, n_orb, node_total,...  41.7 us
    pallas_call x1, Pallas kernels, rotate(): pl.pallas_call(rotate_kernel, out_shape=jax.ShapeDtypeStruct(rows.shape,...  12.8 us
    unnamed x5, local copies, waits for them, and re-layouts  9.82 us

profile of v3, /device:TPU:0, one launch (start us, length us, event | category | flops | bytes accessed | tf_op | source)
XLA Modules:
  0.0 133.9 jit_solution(15256492492048782951)
XLA Ops:
  0.7 8.8 %copy.9 = f32[1,4,729,729]{3,2,1,0:T(8,128)} copy(f32[1,4,729,729]{3,1,2,0:T(4,128)} %param.7) | data formatting | bytes 17006112 | tf_op args[1]
  9.4 0.0 copy-start.1
  9.4 68.9 %filter.1.field = f32[4,288,128]{2,1,0:T(8,128)} custom-call(f32[96,1536]{1,0:T(8,128)} %bitcast.11, f32[4,729,729]{2,1,0:T(8,128)} %bitcast.10, s32[4,729]{1,0:T(4,128)} %bitcast.12, s32[1,1]{1,0:T(1,128)} %bitcast.9.live, s32[1,512]{1,0:T(1,128)} %lower_list.3, s32[1,512]{1,0:T(1,128)} %upper_list.1), custom_call_target="tpu_custom_call" | custom-call | tf_op jit(solution)/shard_map/filter/pallas_call | solution.py:280
  78.3 0.0 copy-done.1
  78.3 0.0 copy-start
  78.3 1.1 copy-done
  79.4 41.7 %turn_and_gram.1 = (f32[384,384]{1,0:T(8,128)S(1)}, f32[768,128]{1,0:T(8,128)S(1)}) custom-call(f32[4,288,128]{2,1,0:T(8,128)S(1)} %copy-done, s32[1,512]{1,0:T(1,128)S(1)} %copy-done.1), custom_call_target="tpu_custom_call" | custom-call | tf_op jit(solution)/shard_map/turn_and_gram/pallas_call | solution.py:409
  121.1 12.8 %rotate.1 = f32[384,384]{1,0:T(8,128)} custom-call(f32[384,384]{1,0:T(8,128)S(1)} %get-tuple-element.7.rows, f32[768,128]{1,0:T(8,128)S(1)} %get-tuple-element.8.gram), custom_call_target="tpu_custom_call" | custom-call | tf_op jit(solution)/shard_map/rotate/pallas_call | solution.py:524
Async XLA Ops:
  9.4 68.9 %copy-start.1 = (s32[1,512]{1,0:T(1,128)S(1)}, s32[1,512]{1,0:T(1,128)}, u32[]{:S(2)}) copy-start(s32[1,512]{1,0:T(1,128)} %lower_list.3) | copy-start | bytes 6148
  78.3 1.1 copy-start
